TPU v7x, 512 devices: a whole 4x4x16 slice. The times are simulated.
512 devices in a mesh: section: 8 (over x, core), sp: 16 (over y, z_hi), cfg: 4 (over z_lo).
Axes of the slice: x: 4, y: 4, z: 16 (z_hi: 4, z_lo: 4; z = z_hi * 4 + z_lo), core: 2. Of those that a mesh axis runs over, the one named last changes fastest.
Arguments:
- queries: bfloat16 [16384, 2048], P(('section', 'sp', 'cfg')), may hold values from -112 to 112
- fresh_keys: bfloat16 [16384, 2048], P(('section', 'sp', 'cfg')), may hold values from -4 to 4
- fresh_values: bfloat16 [16384, 2048], P(('section', 'sp', 'cfg')), may hold values from -6 to 6
- stale_keys: bfloat16 [16, 16384, 128], P('sp', ('section', 'cfg')), may hold values from -6 to 6
- stale_values: bfloat16 [16, 16384, 128], P('sp', ('section', 'cfg')), may hold values from -6 to 6
- text_keys: bfloat16 [512, 2048], P('sp'), may hold values from -6 to 6
- text_values: bfloat16 [512, 2048], P('sp'), may hold values from -6 to 6
- order: int32 [8], replicated, may hold values from 0 to 1023
Outputs:
- attended: bfloat16 [16384, 2048], P(('section', 'sp', 'cfg'))
All inputs are finite; a program needn't handle non-finite values.
Results may differ from a plain program's by a relative error of at most 0.006.
Values may be sent and summed in bfloat16 or wider, within the bound.
A program may use at most 64 MiB of HBM per device.

v0:
```python
import math

import jax
import jax.numpy as jnp
from jax import lax
from jax.sharding import PartitionSpec as P


def online(state, block_keys, block_values, head_queries, score_scale):
    best, total, summed = state
    scores = (
        jnp.einsum("hqe,hke->hqk", head_queries, block_keys, preferred_element_type=jnp.float32)
        * score_scale
    )
    new_best = jnp.maximum(best, jnp.max(scores, axis=-1))
    factor = jnp.exp(best - new_best)
    weights = jnp.exp(scores - new_best[..., None])
    total = total * factor + jnp.sum(weights, axis=-1)
    summed = summed * factor[..., None] + jnp.einsum(
        "hqk,hke->hqe",
        weights.astype(jnp.bfloat16),
        block_values,
        preferred_element_type=jnp.float32,
    )
    return (new_best, total, summed)


def local(
    queries, fresh_keys, fresh_values, stale_keys, stale_values, text_keys, text_values, order
):
    local_heads, shard_rows, head_size = stale_keys.shape
    score_scale = 1.0 / math.sqrt(head_size)
    mixed = (
        lax.all_to_all(queries, "sp", split_axis=1, concat_axis=0, tiled=True),
        lax.all_to_all(fresh_keys, "sp", split_axis=1, concat_axis=0, tiled=True),
        lax.all_to_all(fresh_values, "sp", split_axis=1, concat_axis=0, tiled=True),
        lax.all_to_all(text_keys, "sp", split_axis=1, concat_axis=0, tiled=True),
        lax.all_to_all(text_values, "sp", split_axis=1, concat_axis=0, tiled=True),
    )

    def by_head(matrix):
        return matrix.reshape(matrix.shape[0], local_heads, head_size).transpose(1, 0, 2)

    own_queries, own_keys, own_values, txt_keys, txt_values = [by_head(item) for item in mixed]
    sections = lax.axis_size("section")
    mine = lax.axis_index("section")
    places = jnp.arange(sections, dtype=jnp.int32)
    my_rank = jnp.sum(jnp.where(places == mine, order, 0))
    fresh_for = (my_rank <= order)[:, None, None, None]
    slot_keys = jnp.where(fresh_for, own_keys[None], stale_keys[None])
    slot_values = jnp.where(fresh_for, own_values[None], stale_values[None])
    chosen_keys, chosen_values = (
        lax.all_to_all(slot_keys, "section", split_axis=0, concat_axis=0, tiled=True),
        lax.all_to_all(slot_values, "section", split_axis=0, concat_axis=0, tiled=True),
    )
    query_rows = own_queries.shape[1]
    initial = (
        jnp.full((local_heads, query_rows), -jnp.inf, jnp.float32),
        jnp.zeros((local_heads, query_rows), jnp.float32),
        jnp.zeros((local_heads, query_rows, head_size), jnp.float32),
    )
    initial = online(initial, txt_keys, txt_values, own_queries, score_scale)
    state = initial
    piece_keys = lax.all_gather(chosen_keys, "cfg", axis=2, tiled=True)
    piece_values = lax.all_gather(chosen_values, "cfg", axis=2, tiled=True)
    key_rows = piece_keys.shape[2]
    block_rows = 1024
    several = key_rows // block_rows

    def arrange(tensor):
        split = tensor.reshape(tensor.shape[0], local_heads, several, block_rows, head_size)
        return split.transpose(0, 2, 1, 3, 4).reshape(
            tensor.shape[0] * several, local_heads, block_rows, head_size
        )

    def advance(carry, pair):
        return (online(carry, pair[0], pair[1], own_queries, score_scale), None)

    state, unused = lax.scan(advance, state, (arrange(piece_keys), arrange(piece_values)))
    best, total, summed = state
    result = (summed / total[..., None]).astype(jnp.bfloat16)
    merged = result.transpose(1, 0, 2).reshape(query_rows, local_heads * head_size)
    return lax.all_to_all(merged, "sp", split_axis=0, concat_axis=1, tiled=True)


def solution(mesh):
    return jax.shard_map(
        local,
        mesh=mesh,
        in_specs=(
            P(("section", "sp", "cfg"), None),
            P(("section", "sp", "cfg"), None),
            P(("section", "sp", "cfg"), None),
            P("sp", ("section", "cfg"), None),
            P("sp", ("section", "cfg"), None),
            P("sp", None),
            P("sp", None),
            P(),
        ),
        out_specs=P(("section", "sp", "cfg"), None),
        check_vma=False,
    )
```

profile of v0, /device:TPU:1, one launch (start us, length us, event | category | flops | bytes accessed | tf_op | source)
XLA Modules:
  0.0 362.4 jit_solution(15010649231298320541)
XLA Ops:
  8.1 18.4 %all-to-all-start.3 = ((bf16[32,16,128]{2,0,1:T(8,128)(2,1)}), bf16[32,16,128]{2,0,1:T(8,128)(2,1)S(1)}, u32[]{:S(2)}, u32[]{:S(2)}) async-start(bf16[32,16,128]{2,0,1:T(8,128)(2,1)} %copy_bitcast_fusion.2), calls=%async_computation.3 | async-start | bytes 262144 | tf_op jit(solution)/shard_map/all_to_all | solution.py:35
  26.5 1.6 copy_bitcast_fusion.1
  28.1 14.1 %all-to-all-done.3 = bf16[32,16,128]{2,0,1:T(8,128)(2,1)S(1)} async-done(((bf16[32,16,128]{2,0,1:T(8,128)(2,1)}), bf16[32,16,128]{2,0,1:T(8,128)(2,1)S(1)}, u32[]{:S(2)}, u32[]{:S(2)}) %all-to-all-start.3) | async-done | bytes 131104 | tf_op jit(solution)/shard_map/all_to_all | solution.py:35
  42.2 3.6 %all-to-all-start.5 = ((bf16[32,16,128]{2,0,1:T(8,128)(2,1)}), bf16[32,16,128]{2,0,1:T(8,128)(2,1)S(1)}, u32[]{:S(2)}, u32[]{:S(2)}) async-start(bf16[32,16,128]{2,0,1:T(8,128)(2,1)} %copy_bitcast_fusion.1), calls=%async_computation.5 | async-start | bytes 262144 | tf_op jit(solution)/shard_map/all_to_all | solution.py:36
  48.5 11.6 %all-to-all-done.5 = bf16[32,16,128]{2,0,1:T(8,128)(2,1)S(1)} async-done(((bf16[32,16,128]{2,0,1:T(8,128)(2,1)}), bf16[32,16,128]{2,0,1:T(8,128)(2,1)S(1)}, u32[]{:S(2)}, u32[]{:S(2)}) %all-to-all-start.5) | async-done | bytes 131104 | tf_op jit(solution)/shard_map/all_to_all | solution.py:36
  61.3 22.9 %all_to_all.109 = bf16[8,1,512,128]{3,2,1,0:T(8,128)(2,1)} all-to-all(bf16[8,1,512,128]{3,2,1,0:T(8,128)(2,1)S(1)} %get-tuple-element.78), channel_id=1, replica_groups=mesh['section'=8,'sp'=16,'cfg'=4] {'section'}, dimensions={0} | all-to-all | bytes 2097152 | tf_op jit(solution)/shard_map/all_to_all | solution.py:53
  84.3 19.3 %all_to_all.110 = bf16[8,1,512,128]{3,2,1,0:T(8,128)(2,1)} all-to-all(bf16[8,1,512,128]{3,2,1,0:T(8,128)(2,1)S(1)} %get-tuple-element.77), channel_id=1, replica_groups=mesh['section'=8,'sp'=16,'cfg'=4] {'section'}, dimensions={0} | all-to-all | bytes 2097152 | tf_op jit(solution)/shard_map/all_to_all | solution.py:54
  104.4 4.6 %all-to-all-start = ((bf16[32,16,128]{2,0,1:T(8,128)(2,1)}), bf16[32,16,128]{2,0,1:T(8,128)(2,1)S(1)}, u32[]{:S(2)}, u32[]{:S(2)}) async-start(bf16[32,16,128]{2,0,1:T(8,128)(2,1)} %copy_bitcast_fusion.5), calls=%async_computation | async-start | bytes 262144 | tf_op jit(solution)/shard_map/all_to_all | solution.py:34
  109.7 16.4 %all-to-all-done = bf16[32,16,128]{2,0,1:T(8,128)(2,1)S(1)} async-done(((bf16[32,16,128]{2,0,1:T(8,128)(2,1)}), bf16[32,16,128]{2,0,1:T(8,128)(2,1)S(1)}, u32[]{:S(2)}, u32[]{:S(2)}) %all-to-all-start) | async-done | bytes 131104 | tf_op jit(solution)/shard_map/all_to_all | solution.py:34
  126.1 3.5 all-to-all-start.1
  130.3 15.8 %all-to-all-done.1 = bf16[32,16,128]{2,0,1:T(8,128)(2,1)S(1)} async-done(((bf16[32,16,128]{2,0,1:T(8,128)(2,1)}), bf16[32,16,128]{2,0,1:T(8,128)(2,1)S(1)}, u32[]{:S(2)}, u32[]{:S(2)}) %all-to-all-start.1) | async-done | bytes 131104 | tf_op jit(solution)/shard_map/all_to_all | solution.py:37
  146.1 3.5 all-to-all-start.2
  150.1 15.7 %all-to-all-done.2 = bf16[32,16,128]{2,0,1:T(8,128)(2,1)S(1)} async-done(((bf16[32,16,128]{2,0,1:T(8,128)(2,1)}), bf16[32,16,128]{2,0,1:T(8,128)(2,1)S(1)}, u32[]{:S(2)}, u32[]{:S(2)}) %all-to-all-start.2) | async-done | bytes 131104 | tf_op jit(solution)/shard_map/all_to_all | solution.py:38
  166.2 14.9 %all-gather.3.cloned.1.call-done = bf16[8,1,2048,128]{3,2,1,0:T(8,128)(2,1)} async-done(((bf16[8,1,512,128]{3,2,1,0:T(8,128)(2,1)}), bf16[8,1,2048,128]{3,2,1,0:T(8,128)(2,1)}) %all-gather.3.cloned.1.call-update) | async-done | bytes 4194320 | tf_op jit(solution)/shard_map/all_gather | solution.py:64
  181.1 91.2 %all-gather.5.cloned.1.call-done = bf16[8,1,2048,128]{3,2,1,0:T(8,128)(2,1)} async-done(((bf16[8,1,512,128]{3,2,1,0:T(8,128)(2,1)}), bf16[8,1,2048,128]{3,2,1,0:T(8,128)(2,1)}) %all-gather.5.cloned.1.call-update) | async-done | bytes 4194320 | tf_op jit(solution)/shard_map/all_gather | solution.py:65
  272.3 53.7 %while.14 = (s32[]{:T(128)}, f32[1,512]{1,0:T(1,128)S(1)}, f32[1,512]{1,0:T(1,128)S(1)}, f32[1,512,128]{2,1,0:T(8,128)S(1)}, bf16[16,1,1024,128]{3,2,1,0:T(8,128...) while((s32[]{:T(128)}, f32[1,512]{1,0:T(1,128)S(1)}, ...), condition=%wide.region_6.7_spmd, body=%wide.region_3.6_spmd.sunk | while | flops 272761856 | bytes 7504981 | solution.py:79
  274.2 1.5 fusion.38
  277.5 1.5 fusion.38
  280.9 1.5 fusion.38
  284.2 1.5 fusion.38
  287.6 1.5 fusion.38
  291.0 1.5 fusion.38
  294.3 1.5 fusion.38
  297.7 1.5 fusion.38
  301.0 1.5 fusion.38
  304.4 1.5 fusion.38
  307.8 1.5 fusion.38
  311.1 1.5 fusion.38
  314.5 1.5 fusion.38
  317.8 1.5 fusion.38
  321.2 1.5 fusion.38
  326.2 28.6 %all_to_all.111 = bf16[16,32,128]{2,1,0:T(8,128)(2,1)S(1)} all-to-all(bf16[16,32,128]{2,1,0:T(8,128)(2,1)S(1)} %bitcast.109), channel_id=1, replica_groups=mesh['section'=8,'sp'=16,'cfg'=4] {'sp'}, dimensions={0} | all-to-all | bytes 262144 | tf_op jit(solution)/shard_map/all_to_all | solution.py:83
  (107 shorter events, 40.0 us)
Async XLA Ops:
  6.5 0.9 copy-start
  8.1 34.1 %all-to-all-start.3 = ((bf16[32,16,128]{2,0,1:T(8,128)(2,1)}), bf16[32,16,128]{2,0,1:T(8,128)(2,1)S(1)}, u32[]{:S(2)}, u32[]{:S(2)}) async-start(bf16[32,16,128]{2,0,1:T(8,128)(2,1)} %copy_bitcast_fusion.2), calls=%async_computation.3 | async-start | bytes 262144 | tf_op jit(solution)/shard_map/all_to_all | solution.py:35
  42.2 17.9 %all-to-all-start.5 = ((bf16[32,16,128]{2,0,1:T(8,128)(2,1)}), bf16[32,16,128]{2,0,1:T(8,128)(2,1)S(1)}, u32[]{:S(2)}, u32[]{:S(2)}) async-start(bf16[32,16,128]{2,0,1:T(8,128)(2,1)} %copy_bitcast_fusion.1), calls=%async_computation.5 | async-start | bytes 262144 | tf_op jit(solution)/shard_map/all_to_all | solution.py:36
  45.8 135.3 %all-gather.3.cloned.1.call-start = ((), (), s32[]{:S(2)}) async-start(), calls=%async_computation.8 | async-start | bytes 5242880 | tf_op jit(solution)/shard_map/all_gather | solution.py:64
  84.2 19.5 %copy-start.1 = (bf16[32,2048]{1,0:T(8,128)(2,1)S(1)}, bf16[32,2048]{1,0:T(8,128)(2,1)}, u32[]{:S(2)}) copy-start(bf16[32,2048]{1,0:T(8,128)(2,1)} %param.10) | copy-start | bytes 393220
  84.2 24.7 %copy-start.2 = (bf16[32,2048]{1,0:T(8,128)(2,1)S(1)}, bf16[32,2048]{1,0:T(8,128)(2,1)}, u32[]{:S(2)}) copy-start(bf16[32,2048]{1,0:T(8,128)(2,1)} %param.15) | copy-start | bytes 393220
  84.2 188.1 %all-gather.5.cloned.1.call-start = ((), (), s32[]{:S(2)}) async-start(), calls=%async_computation.9 | async-start | bytes 5242880 | tf_op jit(solution)/shard_map/all_gather | solution.py:65
  84.3 45.3 %copy-start.3 = (bf16[32,2048]{1,0:T(8,128)(2,1)S(1)}, bf16[32,2048]{1,0:T(8,128)(2,1)}, u32[]{:S(2)}) copy-start(bf16[32,2048]{1,0:T(8,128)(2,1)} %param.16) | copy-start | bytes 393220
  104.4 21.7 %all-to-all-start = ((bf16[32,16,128]{2,0,1:T(8,128)(2,1)}), bf16[32,16,128]{2,0,1:T(8,128)(2,1)S(1)}, u32[]{:S(2)}, u32[]{:S(2)}) async-start(bf16[32,16,128]{2,0,1:T(8,128)(2,1)} %copy_bitcast_fusion.5), calls=%async_computation | async-start | bytes 262144 | tf_op jit(solution)/shard_map/all_to_all | solution.py:34
  126.1 20.0 %all-to-all-start.1 = ((bf16[32,16,128]{2,0,1:T(8,128)(2,1)}), bf16[32,16,128]{2,0,1:T(8,128)(2,1)S(1)}, u32[]{:S(2)}, u32[]{:S(2)}) async-start(bf16[32,16,128]{2,0,1:T(8,128)(2,1)} %copy_bitcast_fusion.4), calls=%async_computation.1 | async-start | bytes 262144 | tf_op jit(solution)/shard_map/all_to_all | solution.py:37
  146.1 19.7 %all-to-all-start.2 = ((bf16[32,16,128]{2,0,1:T(8,128)(2,1)}), bf16[32,16,128]{2,0,1:T(8,128)(2,1)S(1)}, u32[]{:S(2)}, u32[]{:S(2)}) async-start(bf16[32,16,128]{2,0,1:T(8,128)(2,1)} %copy_bitcast_fusion.3), calls=%async_computation.2 | async-start | bytes 262144 | tf_op jit(solution)/shard_map/all_to_all | solution.py:38
Sparse Core Ops, SparseCore 0:
  84.4 96.7 all-gather.2
  183.2 89.0 all-gather.4
where the time goes:
time: 365 us; the launch traced here: 362 us
  waiting for transfers between devices  180 us (49%)
  blocking collectives  70.8 us (19%)
  matrix products  47 us (13%)
  starting transfers between devices  33.7 us (9%)
  between operations  13.5 us (4%)
  other arithmetic  11 us (3%)
  local copies, waits for them, and re-layouts  5.93 us (2%)
    all_gather x1, waiting for transfers between devices, local(): piece_values = lax.all_gather(chosen_values, 'cfg', axis=2, tiled=True)  91.2 us
    all_to_all x1, blocking collectives, local(): return lax.all_to_all(merged, 'sp', split_axis=0, concat_axis=1, tiled=True)  28.6 us
    dot_general x17, matrix products, online(): jnp.einsum('hqk,hke->hqe', weights.astype(jnp.bfloat16), block_values, pr...  24.4 us
    all_to_all x1, blocking collectives, local(): lax.all_to_all(slot_keys, 'section', split_axis=0, concat_axis=0, tiled=T...  22.9 us
    dot_general x17, matrix products, online(): jnp.einsum('hqe,hke->hqk', head_queries, block_keys, preferred_element_ty...  22.6 us
    all_to_all x1, blocking collectives, local(): lax.all_to_all(slot_values, 'section', split_axis=0, concat_axis=0, tiled...  19.3 us
    all_to_all x1, starting transfers between devices, local(): lax.all_to_all(fresh_keys, 'sp', split_axis=1, concat_axis=0, tiled=True)  18.4 us
    all_to_all x1, waiting for transfers between devices, local(): lax.all_to_all(queries, 'sp', split_axis=1, concat_axis=0, tiled=True)  16.4 us
  transfers between devices with their start and end apart: 7, of which 7 were waited for; matrix products, arithmetic and copies ran while one was open for 2% of the time, Pallas kernels for 0%

commit v1 on v0

v1 whole, which is shorter than its diff:
```python
import math

import jax
import jax.numpy as jnp
from jax import lax
from jax.experimental import pallas as pl
from jax.experimental.pallas import tpu as pltpu
from jax.sharding import PartitionSpec as P

MESH = pl.DeviceIdType.MESH
HD = 128
ROWS = 32
GROUP = 512
SEC = 8
TXT = 128
KEYS = SEC * GROUP + TXT
TILE = 256
SCALE2 = math.log2(math.e) / math.sqrt(HD)


def kernel(
    q_in, fk_in, fv_in, sk_in, sv_in, tk_in, tv_in, order,
    out,
    qg, fresh, stale, text, keys2, vals2, q2, sbuf, part, stats, got, got_stats, own, own_l, merged,
    sem_send, sem_q, sem_k, sem_v, sem_text, sem_stale, sem_xs, sem_xf, sem_cs, sem_cf, sem_y, sem_part, sem_stats,
    sem_out,
):
    sec = lax.axis_index("section")
    sp = lax.axis_index("sp")
    low = lax.axis_index("cfg")
    x, core = sec // 2, sec % 2
    y, high = sp // 4, sp % 4
    z = high * 4 + low

    def at_z(zz):
        return (sec, y * 4 + zz // 4, zz % 4)

    def at_y(yy):
        return (sec, yy * 4 + high, low)

    def at_sec(ss):
        return (ss, sp, low)

    def cols(head):
        return pl.ds(pl.multiple_of(head * HD, HD), HD)

    def rows(start, size):
        return pl.ds(pl.multiple_of(start, size), size)

    def head_of(zz):
        return (zz % 4) * 4 + zz // 4

    def remote(src, dst, recv, target):
        copy = pltpu.make_async_remote_copy(
            src_ref=src, dst_ref=dst, send_sem=sem_send.at[0], recv_sem=recv, device_id=target, device_id_type=MESH
        )
        copy.start()

    def arrived(ref, sem):
        pltpu.make_async_copy(ref, ref, sem).wait()

    sibling = sec + 1 - 2 * core
    across = [lax.rem(x + d, 4) * 2 + core for d in range(1, 4)]

    barrier = pltpu.get_barrier_semaphore()

    def greet(target):
        pl.semaphore_signal(barrier, inc=1, device_id=target, device_id_type=MESH)

    for d in (8, 7, 9, 6, 10, 5, 11, 4, 12, 3, 13, 2, 14, 1, 15):
        greet(at_z(lax.rem(z + d, 16)))
    for d in range(1, 4):
        greet(at_y(lax.rem(y + d, 4)))
    for s in across:
        greet(at_sec(s))
    greet(at_sec(sibling))

    @pl.when(low != y)
    def _():
        for c in range(4):
            greet((sec, low * 4 + high, c))

    pl.semaphore_wait(barrier, 25)

    for kv, src in enumerate((sk_in, sv_in)):
        for k in range(1, 4):
            r = lax.rem(y + k, 4)
            remote(src.at[0, rows(r * 128, 128)], stale.at[sec, kv, rows(low * 128, 128)], sem_stale.at[0], (sec, r * 4 + high, y))

        @pl.when(low != y)
        def _():
            remote(src.at[0, rows(y * 128, 128)], stale.at[sec, kv, rows(low * 128, 128)], sem_stale.at[0], (sec, sp, y))

        @pl.when(low == y)
        def _():
            pltpu.make_async_copy(src.at[0, rows(y * 128, 128)], stale.at[sec, kv, rows(low * 128, 128)], sem_stale.at[0]).start()

    mine = cols(head_of(z))
    place = rows(z * ROWS, ROWS)
    for src, dst, sem in ((fk_in, fresh.at[sec, 0], sem_k), (fv_in, fresh.at[sec, 1], sem_v), (q_in, qg.at[y], sem_q)):
        pltpu.make_async_copy(src.at[:, mine], dst.at[place], sem.at[0]).start()
        for d in (8, 7, 9, 6, 10, 5, 11, 4, 12, 3, 13, 2, 14, 1, 15):
            zz = lax.rem(z + d, 16)
            remote(src.at[:, cols(head_of(zz))], dst.at[place], sem.at[0], at_z(zz))
    text_place = rows(high * ROWS, ROWS)
    for kv, src in enumerate((tk_in, tv_in)):
        pltpu.make_async_copy(src.at[:, mine], text.at[kv, text_place], sem_text.at[0]).start()
        for d in (2, 1, 3):
            a = lax.rem(high + d, 4)
            remote(src.at[:, cols(low * 4 + a)], text.at[kv, text_place], sem_text.at[0], (sec, y * 4 + a, low))

    def spread(block, sem_x, sem_c):
        for i, s in enumerate(across):
            remote(block.at[sec], block.at[sec], sem_x.at[i], at_sec(s))
        remote(block.at[sec], block.at[sec], sem_c.at[3], at_sec(sibling))

    def forward(block, sem_x, sem_c):
        for i in (0, 2, 1):
            s = lax.rem(x + 3 - i, 4) * 2 + core
            arrived(block.at[s], sem_x.at[i])
            remote(block.at[s], block.at[s], sem_c.at[i], at_sec(sibling))

    arrived(stale.at[sec], sem_stale.at[0])
    spread(stale, sem_xs, sem_cs)
    arrived(fresh.at[sec, 0], sem_k.at[0])
    arrived(fresh.at[sec, 1], sem_v.at[0])
    spread(fresh, sem_xf, sem_cf)
    arrived(qg.at[y], sem_q.at[0])
    for k in range(1, 4):
        remote(qg.at[y], qg.at[y], sem_y.at[k - 1], at_y(lax.rem(y + k, 4)))
    forward(stale, sem_xs, sem_cs)
    arrived(text, sem_text.at[0])
    vals2[:, HD:] = jnp.ones((KEYS, HD), jnp.bfloat16)
    keys2[SEC * GROUP :, :HD] = text[0]
    keys2[SEC * GROUP :, HD:] = text[0]
    vals2[SEC * GROUP :, :HD] = text[1]
    forward(fresh, sem_xf, sem_cf)
    for i in range(4):
        s = lax.rem(x + 3 - i + 4, 4) * 2 + 1 - core
        arrived(stale.at[s], sem_cs.at[i])
        arrived(fresh.at[s], sem_cf.at[i])

    my_order = order[sec]
    for j in range(SEC):
        use_fresh = order[j] <= my_order
        block = pl.ds(j * GROUP, GROUP)
        chosen = jnp.where(use_fresh, fresh[j, 0], stale[j, 0])
        keys2[block, :HD] = chosen
        keys2[block, HD:] = chosen
        vals2[block, :HD] = jnp.where(use_fresh, fresh[j, 1], stale[j, 1])

    def scaled(yy):
        wide = qg[yy].astype(jnp.float32) * SCALE2
        first = wide.astype(jnp.bfloat16)
        q2[yy, :, :HD] = first
        q2[yy, :, HD:] = (wide - first.astype(jnp.float32)).astype(jnp.bfloat16)

    scaled(y)
    for k in range(1, 4):
        yy = lax.rem(y + 4 - k, 4)
        arrived(qg.at[yy], sem_y.at[k - 1])
        scaled(yy)

    def tile_of(t):
        return lax.rem(y + 1 + t, 4), t // 4

    def scores(t):
        yy, half = tile_of(t)
        return lax.dot_general(
            q2[yy, rows(half * TILE, TILE), :], keys2[...], (((1,), (1,)), ((), ())), preferred_element_type=jnp.float32
        )

    def finish(t, s):
        yy, half = tile_of(t)
        best = jnp.max(s, axis=1, keepdims=True)
        weights = jnp.exp2(s - best).astype(jnp.bfloat16)
        both = jnp.dot(weights, vals2[...], preferred_element_type=jnp.float32)
        total = both[:, HD:]
        value = both[:, :HD] / total
        level = best + jnp.log2(total)
        return yy, half, value, level

    def give(t, s):
        yy, half, value, level = finish(t, s)
        part[yy, rows(half * TILE, TILE), :] = value.astype(jnp.bfloat16)
        stats[yy, half] = jnp.transpose(level)[:8]
        remote(part.at[yy, rows(half * TILE, TILE)], got.at[y, rows(half * TILE, TILE)], sem_part.at[half, y], at_y(yy))
        remote(stats.at[yy, half], got_stats.at[y, half], sem_stats.at[half, y], at_y(yy))

    def keep(t, s):
        yy, half, value, level = finish(t, s)
        own[half] = value
        own_l[half] = level

    def merge(half):
        here = rows(half * TILE, TILE)
        levels, values = [own_l[half]], [own[half]]
        for k in range(1, 4):
            yy = lax.rem(y + k, 4)
            arrived(got.at[yy, here], sem_part.at[half, yy])
            arrived(got_stats.at[yy, half], sem_stats.at[half, yy])
            level = got_stats[yy, half]
            levels.append(jnp.transpose(jnp.broadcast_to(level[:1], (HD, TILE))))
            values.append(got[yy, here, :].astype(jnp.float32))
        top = jnp.maximum(jnp.maximum(levels[0], levels[1]), jnp.maximum(levels[2], levels[3]))
        shares = [jnp.exp2(level - top) for level in levels]
        total = shares[0] + shares[1] + shares[2] + shares[3]
        summed = shares[0] * values[0] + shares[1] * values[1] + shares[2] * values[2] + shares[3] * values[3]
        merged[here, :] = (summed / total).astype(jnp.bfloat16)
        for d in range(8):
            zz = half * 8 + d
            src = merged.at[rows(zz * ROWS, ROWS)]

            @pl.when(zz == z)
            def _():
                pltpu.make_async_copy(src, out.at[:, mine], sem_out.at[0]).start()

            @pl.when(zz != z)
            def _():
                remote(src, out.at[:, mine], sem_out.at[0], at_z(zz))

    sbuf[0] = scores(0)

    def pair(u, _):
        @pl.when(u == 3)
        def _():
            merge(0)

        t = u * 2
        sbuf[1] = scores(t + 1)
        give(t, sbuf[0])
        sbuf[0] = scores(jnp.minimum(t + 2, 7))

        @pl.when(u % 2 == 0)
        def _():
            give(t + 1, sbuf[1])

        @pl.when(u % 2 == 1)
        def _():
            keep(t + 1, sbuf[1])

        return 0

    lax.fori_loop(0, 4, pair, 0)
    merge(1)

    arrived(out, sem_out.at[0])

    def sent(ref):
        pltpu.make_async_copy(ref, ref, sem_send.at[0]).wait()

    sent(stale.at[0, :, pl.ds(0, 384)])

    @pl.when(low != y)
    def _():
        sent(stale.at[0, :, pl.ds(0, 128)])

    for _ in range(4):
        sent(qg.at[0, pl.ds(0, 480)])
    sent(text.at[:, pl.ds(0, 96)])
    for _ in range(14):
        sent(stale.at[0])
    for _ in range(3):
        sent(qg.at[0])
    for _ in range(3):
        sent(qg.at[0])
        sent(stats.at[0])


def local(queries, fresh_keys, fresh_values, stale_keys, stale_values, text_keys, text_values, order):
    anywhere = pl.BlockSpec(memory_space=pl.ANY)
    dma = pltpu.SemaphoreType.DMA
    bf16, f32 = jnp.bfloat16, jnp.float32
    return pl.pallas_call(
        kernel,
        out_shape=jax.ShapeDtypeStruct((ROWS, 16 * HD), bf16),
        in_specs=[anywhere] * 7 + [pl.BlockSpec(memory_space=pltpu.SMEM)],
        out_specs=anywhere,
        scratch_shapes=[
            pltpu.VMEM((4, GROUP, HD), bf16),
            pltpu.VMEM((SEC, 2, GROUP, HD), bf16),
            pltpu.VMEM((SEC, 2, GROUP, HD), bf16),
            pltpu.VMEM((2, TXT, HD), bf16),
            pltpu.VMEM((KEYS, 2 * HD), bf16),
            pltpu.VMEM((KEYS, 2 * HD), bf16),
            pltpu.VMEM((4, GROUP, 2 * HD), bf16),
            pltpu.VMEM((2, TILE, KEYS), f32),
            pltpu.VMEM((4, GROUP, HD), bf16),
            pltpu.VMEM((4, 2, 8, TILE), f32),
            pltpu.VMEM((4, GROUP, HD), bf16),
            pltpu.VMEM((4, 2, 8, TILE), f32),
            pltpu.VMEM((2, TILE, HD), f32),
            pltpu.VMEM((2, TILE, HD), f32),
            pltpu.VMEM((GROUP, HD), bf16),
            dma((1,)),
            dma((1,)),
            dma((1,)),
            dma((1,)),
            dma((1,)),
            dma((1,)),
            dma((3,)),
            dma((3,)),
            dma((4,)),
            dma((4,)),
            dma((3,)),
            dma((2, 4)),
            dma((2, 4)),
            dma((1,)),
        ],
        compiler_params=pltpu.CompilerParams(collective_id=0, has_side_effects=True, vmem_limit_bytes=56 << 20),
    )(queries, fresh_keys, fresh_values, stale_keys, stale_values, text_keys, text_values, order)


def solution(mesh):
    return jax.shard_map(
        local,
        mesh=mesh,
        in_specs=(
            P(("section", "sp", "cfg"), None),
            P(("section", "sp", "cfg"), None),
            P(("section", "sp", "cfg"), None),
            P("sp", ("section", "cfg"), None),
            P("sp", ("section", "cfg"), None),
            P("sp", None),
            P("sp", None),
            P(),
        ),
        out_specs=P(("section", "sp", "cfg"), None),
        check_vma=False,
    )
```

time: 365 us -> 98.4 us (0.27)
  waiting for transfers between devices: 180 us -> 0 us
  Pallas kernels: 0 us -> 96.7 us
  blocking collectives: 70.8 us -> 0 us
  matrix products: 47 us -> 0 us
  starting transfers between devices: 33.7 us -> 0 us
  between operations: 13.5 us -> 0.01 us
  other arithmetic: 11 us -> 0 us
  local copies, waits for them, and re-layouts: 5.93 us -> 1.57 us
    all_gather x2 -> x0, waiting for transfers between devices: 106 us -> none  [the longest x1 91.2 us: local(): piece_values = lax.all_gather(chosen_values, 'cfg', axis=2, tiled=True)]
    pallas_call x0 -> x1, Pallas kernels: none -> 96.7 us  [local(): pl.pallas_call(kernel, out_shape=jax.ShapeDtypeStruct((ROWS, 16 * HD), bf...]
    all_to_all x5 -> x0, waiting for transfers between devices: 73.6 us -> none  [the longest x1 16.4 us: local(): lax.all_to_all(queries, 'sp', split_axis=1, concat_axis=0, tiled=True)]
    all_to_all x3 -> x0, blocking collectives: 70.8 us -> none  [the longest x1 28.6 us: local(): return lax.all_to_all(merged, 'sp', split_axis=0, concat_axis=1, tiled=True)]
    dot_general x34 -> x0, matrix products: 47 us -> none  [the longest x17 24.4 us: online(): jnp.einsum('hqk,hke->hqe', weights.astype(jnp.bfloat16), block_values, pr...]
    all_to_all x5 -> x0, starting transfers between devices: 33.6 us -> none  [the longest x1 18.4 us: local(): lax.all_to_all(fresh_keys, 'sp', split_axis=1, concat_axis=0, tiled=True)]
    reduce_sum x18 -> x0, other arithmetic: 7.93 us -> none  [the longest x17 6.61 us: online(): total = total * factor + jnp.sum(weights, axis=-1)]
    all_to_all x6 -> x0, local copies, waits for them, and re-layouts: 4.97 us -> none  [the longest x1 1.58 us: local(): lax.all_to_all(fresh_values, 'sp', split_axis=1, concat_axis=0, tiled=True)]
  transfers between devices with their start and end apart: 7 -> 0, of which waited for: 7 -> 0; matrix products, arithmetic and copies ran while one was open for 2% -> 0% of each run, Pallas kernels for 0% -> 0%
where the time goes in v1:
time: 98.4 us; the launch traced here: 98.2 us
  Pallas kernels  96.7 us (98%)
  local copies, waits for them, and re-layouts  1.57 us (2%)
    pallas_call x1, Pallas kernels, local(): pl.pallas_call(kernel, out_shape=jax.ShapeDtypeStruct((ROWS, 16 * HD), bf...  96.7 us

profile of v1, /device:TPU:1, one launch (start us, length us, event | category | flops | bytes accessed | tf_op | source)
XLA Modules:
  0.0 98.2 jit_solution(15673653706831986262)
XLA Ops:
  0.0 96.7 %shard_map.82 = bf16[32,2048]{1,0:T(8,128)(2,1)} custom-call(bf16[32,2048]{1,0:T(8,128)(2,1)} %q_in.1, bf16[32,2048]{1,0:T(8,128)(2,1)} %fk_in.1, bf16[32,2048]{1,0:T(8,128)(2,1)} %fv_in.1, bf16[1,512,128]{2,1,0:T(8,128)(2,1)} %sk_in.1, bf16[1,512,128]{2,1,0:T(8,128)(2,1)} %sv_in.1, bf16[32,2048]{1,0:T(8,128)(2,1)} %tk_in.1, bf16[32,2048]{1,0:T(8,128)(2,1)} %tv_in.1, ...), custom_call_target="tpu_custom_call" | custom-call | tf_op jit(solution)/shard_map/pallas_call | solution.py:274
  96.7 1.6 %copy.10 = bf16[32,2048]{1,0:T(8,128)(2,1)} copy(bf16[32,2048]{1,0:T(8,128)(2,1)} %shard_map.82) | data formatting | bytes 262144

commit v2 on v1

--- a/solution.py
+++ b/solution.py
@@ -14,6 +14,7 @@
 SEC = 8
 TXT = 128
 KEYS = SEC * GROUP + TXT
+FAR_FIRST = (8, 7, 9, 6, 10, 5, 11, 4, 12, 3, 13, 2, 14, 1, 15)
 TILE = 256
 SCALE2 = math.log2(math.e) / math.sqrt(HD)
 
@@ -21,8 +22,8 @@
 def kernel(
     q_in, fk_in, fv_in, sk_in, sv_in, tk_in, tv_in, order,
     out,
-    qg, fresh, stale, text, keys2, vals2, q2, sbuf, part, stats, got, got_stats, own, own_l, merged,
-    sem_send, sem_q, sem_k, sem_v, sem_text, sem_stale, sem_xs, sem_xf, sem_cs, sem_cf, sem_y, sem_part, sem_stats,
+    qg, fresh, stale, hop, text, keys2, vals2, q2, sbuf, part, stats, got, got_stats, own, own_l, merged,
+    sem_send, sem_q, sem_k, sem_v, sem_text, sem_stale, sem_u, sem_hop, sem_y, sem_part, sem_stats,
     sem_out,
 ):
     sec = lax.axis_index("section")
@@ -60,85 +61,148 @@
         pltpu.make_async_copy(ref, ref, sem).wait()
 
     sibling = sec + 1 - 2 * core
-    across = [lax.rem(x + d, 4) * 2 + core for d in range(1, 4)]
+    right, opposite, left = [lax.rem(x + d, 4) * 2 + core for d in range(1, 4)]
 
     barrier = pltpu.get_barrier_semaphore()
 
     def greet(target):
         pl.semaphore_signal(barrier, inc=1, device_id=target, device_id_type=MESH)
 
-    for d in (8, 7, 9, 6, 10, 5, 11, 4, 12, 3, 13, 2, 14, 1, 15):
+    for d in FAR_FIRST:
         greet(at_z(lax.rem(z + d, 16)))
     for d in range(1, 4):
         greet(at_y(lax.rem(y + d, 4)))
-    for s in across:
-        greet(at_sec(s))
+    greet(at_sec(right))
+    greet(at_sec(left))
     greet(at_sec(sibling))
-
-    @pl.when(low != y)
-    def _():
-        for c in range(4):
-            greet((sec, low * 4 + high, c))
-
-    pl.semaphore_wait(barrier, 25)
-
-    for kv, src in enumerate((sk_in, sv_in)):
-        for k in range(1, 4):
-            r = lax.rem(y + k, 4)
-            remote(src.at[0, rows(r * 128, 128)], stale.at[sec, kv, rows(low * 128, 128)], sem_stale.at[0], (sec, r * 4 + high, y))
-
-        @pl.when(low != y)
-        def _():
-            remote(src.at[0, rows(y * 128, 128)], stale.at[sec, kv, rows(low * 128, 128)], sem_stale.at[0], (sec, sp, y))
-
-        @pl.when(low == y)
-        def _():
-            pltpu.make_async_copy(src.at[0, rows(y * 128, 128)], stale.at[sec, kv, rows(low * 128, 128)], sem_stale.at[0]).start()
+    pl.semaphore_wait(barrier, 21)
+
+    for k in (2, 1, 3):
+        r = lax.rem(y + k, 4)
+        for kv, src in enumerate((sk_in, sv_in)):
+            remote(src.at[0, rows(r * 128, 128)], hop.at[y, kv], sem_hop.at[k - 1], at_y(r))
 
     mine = cols(head_of(z))
     place = rows(z * ROWS, ROWS)
-    for src, dst, sem in ((fk_in, fresh.at[sec, 0], sem_k), (fv_in, fresh.at[sec, 1], sem_v), (q_in, qg.at[y], sem_q)):
-        pltpu.make_async_copy(src.at[:, mine], dst.at[place], sem.at[0]).start()
-        for d in (8, 7, 9, 6, 10, 5, 11, 4, 12, 3, 13, 2, 14, 1, 15):
+
+    def to_heads(src, dst, sem, by_distance):
+        pltpu.make_async_copy(src.at[:, mine], dst.at[rows(4 * ROWS, ROWS) if by_distance else place], sem.at[0]).start()
+        for d in FAR_FIRST:
             zz = lax.rem(z + d, 16)
-            remote(src.at[:, cols(head_of(zz))], dst.at[place], sem.at[0], at_z(zz))
+            there = rows((4 - d) % 16 * ROWS, ROWS) if by_distance else place
+            remote(src.at[:, cols(head_of(zz))], dst.at[there], sem.at[0], at_z(zz))
+
+    stale_rows = rows(low * 128, 128)
+
+    def swap():
+        @pl.when(low != y)
+        def _():
+            for kv, src in enumerate((sk_in, sv_in)):
+                remote(src.at[0, rows(y * 128, 128)], stale.at[sec, kv, stale_rows], sem_stale.at[0], (sec, sp, y))
+
+        @pl.when(low == y)
+        def _():
+            for kv, src in enumerate((sk_in, sv_in)):
+                pltpu.make_async_copy(src.at[0, rows(y * 128, 128)], stale.at[sec, kv, stale_rows], sem_stale.at[0]).start()
+
+        for k in (1, 3, 2):
+            yy = lax.rem(y + 4 - k, 4)
+            arrived(hop.at[yy], sem_hop.at[k - 1])
+
+            @pl.when(low != yy)
+            def _():
+                remote(hop.at[yy], stale.at[sec, :, stale_rows], sem_stale.at[0], (sec, sp, yy))
+
+            @pl.when(low == yy)
+            def _():
+                pltpu.make_async_copy(hop.at[yy], stale.at[sec, :, stale_rows], sem_stale.at[0]).start()
+
     text_place = rows(high * ROWS, ROWS)
-    for kv, src in enumerate((tk_in, tv_in)):
-        pltpu.make_async_copy(src.at[:, mine], text.at[kv, text_place], sem_text.at[0]).start()
-        for d in (2, 1, 3):
-            a = lax.rem(high + d, 4)
-            remote(src.at[:, cols(low * 4 + a)], text.at[kv, text_place], sem_text.at[0], (sec, y * 4 + a, low))
-
-    def spread(block, sem_x, sem_c):
-        for i, s in enumerate(across):
-            remote(block.at[sec], block.at[sec], sem_x.at[i], at_sec(s))
-        remote(block.at[sec], block.at[sec], sem_c.at[3], at_sec(sibling))
-
-    def forward(block, sem_x, sem_c):
-        for i in (0, 2, 1):
-            s = lax.rem(x + 3 - i, 4) * 2 + core
-            arrived(block.at[s], sem_x.at[i])
-            remote(block.at[s], block.at[s], sem_c.at[i], at_sec(sibling))
-
+
+    def send_text():
+        for kv, src in enumerate((tk_in, tv_in)):
+            pltpu.make_async_copy(src.at[:, mine], text.at[kv, text_place], sem_text.at[0]).start()
+            for d in (2, 1, 3):
+                a = lax.rem(high + d, 4)
+                remote(src.at[:, cols(low * 4 + a)], text.at[kv, text_place], sem_text.at[0], (sec, y * 4 + a, low))
+
+    upper, lower = pl.ds(0, 256), pl.ds(256, 256)
+    from_left, from_right = left, right
+
+    def spread(part_of, sems):
+        block = part_of(sec)
+        remote(block, block, sems.at[0], at_sec(right))
+        remote(block, block, sems.at[1], at_sec(left))
+        remote(block, block, sems.at[4], at_sec(sibling))
+
+    def forward(part_of, half_of, sems):
+        block = part_of(from_left)
+        arrived(block, sems.at[0])
+        half = half_of(from_left, upper)
+        remote(half, half, sems.at[2], at_sec(right))
+        remote(block, block, sems.at[5], at_sec(sibling))
+        block = part_of(from_right)
+        arrived(block, sems.at[1])
+        half = half_of(from_right, lower)
+        remote(half, half, sems.at[3], at_sec(left))
+        remote(block, block, sems.at[6], at_sec(sibling))
+
+    def forward_far(half_of, sems):
+        half = half_of(opposite, upper)
+        arrived(half, sems.at[2])
+        remote(half, half, sems.at[7], at_sec(sibling))
+        half = half_of(opposite, lower)
+        arrived(half, sems.at[3])
+        remote(half, half, sems.at[8], at_sec(sibling))
+
+    def all_here(part_of, half_of, sems):
+        arrived(part_of(sibling), sems.at[4])
+        arrived(part_of(from_left + other), sems.at[5])
+        arrived(part_of(from_right + other), sems.at[6])
+        arrived(half_of(opposite + other, upper), sems.at[7])
+        arrived(half_of(opposite + other, lower), sems.at[8])
+
+    other = 1 - 2 * core
+    keys_unit = (lambda s: fresh.at[s, 0], lambda s, h: fresh.at[s, 0, h], sem_u.at[0])
+    vals_unit = (lambda s: fresh.at[s, 1], lambda s, h: fresh.at[s, 1, h], sem_u.at[1])
+    stale_unit = (lambda s: stale.at[s], lambda s, h: stale.at[s, :, h], sem_u.at[2])
+
+    def do_spread(unit):
+        spread(unit[0], unit[2])
+
+    def do_forward(unit):
+        forward(*unit)
+
+    def do_far(unit):
+        forward_far(unit[1], unit[2])
+
+    to_heads(fk_in, fresh.at[sec, 0], sem_k, False)
+    to_heads(fv_in, fresh.at[sec, 1], sem_v, False)
+    swap()
+    to_heads(q_in, qg.at[y], sem_q, True)
+    send_text()
+    arrived(fresh.at[sec, 0], sem_k.at[0])
+    do_spread(keys_unit)
     arrived(stale.at[sec], sem_stale.at[0])
-    spread(stale, sem_xs, sem_cs)
-    arrived(fresh.at[sec, 0], sem_k.at[0])
+    do_spread(stale_unit)
     arrived(fresh.at[sec, 1], sem_v.at[0])
-    spread(fresh, sem_xf, sem_cf)
+    do_spread(vals_unit)
+    do_forward(keys_unit)
     arrived(qg.at[y], sem_q.at[0])
-    for k in range(1, 4):
+    for k in (2, 1, 3):
         remote(qg.at[y], qg.at[y], sem_y.at[k - 1], at_y(lax.rem(y + k, 4)))
-    forward(stale, sem_xs, sem_cs)
+    do_forward(stale_unit)
+    do_forward(vals_unit)
+    do_far(keys_unit)
     arrived(text, sem_text.at[0])
     vals2[:, HD:] = jnp.ones((KEYS, HD), jnp.bfloat16)
     keys2[SEC * GROUP :, :HD] = text[0]
     keys2[SEC * GROUP :, HD:] = text[0]
     vals2[SEC * GROUP :, :HD] = text[1]
-    forward(fresh, sem_xf, sem_cf)
-    for i in range(4):
-        s = lax.rem(x + 3 - i + 4, 4) * 2 + 1 - core
-        arrived(stale.at[s], sem_cs.at[i])
-        arrived(fresh.at[s], sem_cf.at[i])
+    do_far(stale_unit)
+    do_far(vals_unit)
+    for unit in (keys_unit, stale_unit, vals_unit):
+        all_here(*unit)
 
     my_order = order[sec]
     for j in range(SEC):
@@ -167,7 +231,7 @@
     def scores(t):
         yy, half = tile_of(t)
         return lax.dot_general(
-            q2[yy, rows(half * TILE, TILE), :], keys2[...], (((1,), (1,)), ((), ())), preferred_element_type=jnp.float32
+            q2[yy, rows((1 - half) * TILE, TILE), :], keys2[...], (((1,), (1,)), ((), ())), preferred_element_type=jnp.float32
         )
 
     def finish(t, s):
@@ -207,17 +271,13 @@
         total = shares[0] + shares[1] + shares[2] + shares[3]
         summed = shares[0] * values[0] + shares[1] * values[1] + shares[2] * values[2] + shares[3] * values[3]
         merged[here, :] = (summed / total).astype(jnp.bfloat16)
-        for d in range(8):
-            zz = half * 8 + d
-            src = merged.at[rows(zz * ROWS, ROWS)]
-
-            @pl.when(zz == z)
-            def _():
+        for d in (0, 7, 1, 6, 2, 5, 3, 4):
+            off = (1 - half) * 8 + d - 4
+            src = merged.at[pl.ds(half * TILE + d * ROWS, ROWS)]
+            if off == 0:
                 pltpu.make_async_copy(src, out.at[:, mine], sem_out.at[0]).start()
-
-            @pl.when(zz != z)
-            def _():
-                remote(src, out.at[:, mine], sem_out.at[0], at_z(zz))
+            else:
+                remote(src, out.at[:, mine], sem_out.at[0], at_z(lax.rem(z + off + 16, 16)))
 
     sbuf[0] = scores(0)
 
@@ -249,12 +309,8 @@
     def sent(ref):
         pltpu.make_async_copy(ref, ref, sem_send.at[0]).wait()
 
-    sent(stale.at[0, :, pl.ds(0, 384)])
-
-    @pl.when(low != y)
-    def _():
-        sent(stale.at[0, :, pl.ds(0, 128)])
-
+    for _ in range(2):
+        sent(stale.at[0, :, pl.ds(0, 384)])
     for _ in range(4):
         sent(qg.at[0, pl.ds(0, 480)])
     sent(text.at[:, pl.ds(0, 96)])
@@ -280,6 +336,7 @@
             pltpu.VMEM((4, GROUP, HD), bf16),
             pltpu.VMEM((SEC, 2, GROUP, HD), bf16),
             pltpu.VMEM((SEC, 2, GROUP, HD), bf16),
+            pltpu.VMEM((4, 2, 128, HD), bf16),
             pltpu.VMEM((2, TXT, HD), bf16),
             pltpu.VMEM((KEYS, 2 * HD), bf16),
             pltpu.VMEM((KEYS, 2 * HD), bf16),
@@ -298,10 +355,8 @@
             dma((1,)),
             dma((1,)),
             dma((1,)),
+            dma((3, 9)),
             dma((3,)),
-            dma((3,)),
-            dma((4,)),
-            dma((4,)),
             dma((3,)),
             dma((2, 4)),
             dma((2, 4)),

time: 98.4 us -> 84.6 us (0.86)
  Pallas kernels: 96.7 us -> 82.9 us
    pallas_call x1, Pallas kernels: 96.7 us -> 82.9 us  [local(): pl.pallas_call(kernel, out_shape=jax.ShapeDtypeStruct((ROWS, 16 * HD), bf...]
where the time goes in v2:
time: 84.6 us; the launch traced here: 84.5 us
  Pallas kernels  82.9 us (98%)
  local copies, waits for them, and re-layouts  1.57 us (2%)
    pallas_call x1, Pallas kernels, local(): pl.pallas_call(kernel, out_shape=jax.ShapeDtypeStruct((ROWS, 16 * HD), bf...  82.9 us

profile of v2, /device:TPU:1, one launch (start us, length us, event | category | flops | bytes accessed | tf_op | source)
XLA Modules:
  0.0 84.5 jit_solution(2388800681920128197)
XLA Ops:
  0.0 82.9 %shard_map.82 = bf16[32,2048]{1,0:T(8,128)(2,1)} custom-call(bf16[32,2048]{1,0:T(8,128)(2,1)} %q_in.1, bf16[32,2048]{1,0:T(8,128)(2,1)} %fk_in.1, bf16[32,2048]{1,0:T(8,128)(2,1)} %fv_in.1, bf16[1,512,128]{2,1,0:T(8,128)(2,1)} %sk_in.1, bf16[1,512,128]{2,1,0:T(8,128)(2,1)} %sv_in.1, bf16[32,2048]{1,0:T(8,128)(2,1)} %tk_in.1, bf16[32,2048]{1,0:T(8,128)(2,1)} %tv_in.1, ...), custom_call_target="tpu_custom_call" | custom-call | tf_op jit(solution)/shard_map/pallas_call | solution.py:330
  82.9 1.6 %copy.10 = bf16[32,2048]{1,0:T(8,128)(2,1)} copy(bf16[32,2048]{1,0:T(8,128)(2,1)} %shard_map.82) | data formatting | bytes 262144

commit v3 on v1

v3 whole, which is shorter than its diff:
```python
import math

import jax
import jax.numpy as jnp
from jax import lax
from jax.experimental import pallas as pl
from jax.experimental.pallas import tpu as pltpu
from jax.sharding import PartitionSpec as P

MESH = pl.DeviceIdType.MESH
HD = 128
ROWS = 32
GROUP = 512
SEC = 8
TXT = 128
KEYS = SEC * GROUP + TXT
HALF = SEC * GROUP // 2
FIRST, SECOND = pl.ds(0, HALF), pl.ds(HALF, HALF + TXT)
FAR_FIRST = (8, 7, 9, 6, 10, 5, 11, 4, 12, 3, 13, 2, 14, 1, 15)
TILE = 256
SCALE2 = math.log2(math.e) / math.sqrt(HD)


def kernel(
    q_in, fk_in, fv_in, sk_in, sv_in, tk_in, tv_in, order,
    out,
    qg, fresh, stale, hop, text, keys2, vals2, q2, sbuf, so_far, best_so_far, partial, stats, got, got_stats, own, own_l, merged,
    sem_send, sem_q, sem_f, sem_text, sem_stale, sem_u, sem_hop, sem_y, sem_part, sem_stats,
    sem_out,
):
    sec = lax.axis_index("section")
    sp = lax.axis_index("sp")
    low = lax.axis_index("cfg")
    x, core = sec // 2, sec % 2
    y, high = sp // 4, sp % 4
    z = high * 4 + low

    def at_z(zz):
        return (sec, y * 4 + zz // 4, zz % 4)

    def at_y(yy):
        return (sec, yy * 4 + high, low)

    def at_sec(ss):
        return (ss, sp, low)

    def cols(head):
        return pl.ds(pl.multiple_of(head * HD, HD), HD)

    def rows(start, size):
        return pl.ds(start if isinstance(start, int) else pl.multiple_of(start, size), size)

    def head_of(zz):
        return (zz % 4) * 4 + zz // 4

    def remote(src, dst, recv, target):
        copy = pltpu.make_async_remote_copy(
            src_ref=src, dst_ref=dst, send_sem=sem_send.at[0], recv_sem=recv, device_id=target, device_id_type=MESH
        )
        copy.start()

    def arrived(ref, sem):
        pltpu.make_async_copy(ref, ref, sem).wait()

    sibling = sec + 1 - 2 * core
    right, opposite, left = [lax.rem(x + d, 4) * 2 + core for d in range(1, 4)]

    barrier = pltpu.get_barrier_semaphore()

    def greet(target):
        pl.semaphore_signal(barrier, inc=1, device_id=target, device_id_type=MESH)

    for d in FAR_FIRST:
        greet(at_z(lax.rem(z + d, 16)))
    for d in range(1, 4):
        greet(at_y(lax.rem(y + d, 4)))
    greet(at_sec(right))
    greet(at_sec(left))
    greet(at_sec(sibling))
    pl.semaphore_wait(barrier, 21)


    pending = {}
    count = [0]

    def units_of(ref):
        n = 1
        for d in ref.shape:
            n *= d
        return n // (ROWS * HD)

    def put(src, dst, recv, target):
        remote(src, dst, recv, target)
        count[0] += units_of(src)

    def expect(name, ref, sem):
        pending[name] = (ref, sem)

    def await_(name):
        arrived(*pending.pop(name))

    for k in (2, 1, 3):
        r = lax.rem(y + k, 4)
        for kv, src in enumerate((sk_in, sv_in)):
            put(src.at[0, rows(r * 128, 128)], hop.at[y, kv], sem_hop.at[k - 1], at_y(r))
        expect(f"hop{k}", hop.at[lax.rem(y + 4 - k, 4)], sem_hop.at[k - 1])

    mine = cols(head_of(z))

    def to_heads(src, dst, sem, distances, place):
        for d in distances:
            if d == 0:
                pltpu.make_async_copy(src.at[:, mine], dst.at[place(d)], sem).start()
            else:
                zz = lax.rem(z + d, 16)
                put(src.at[:, cols(head_of(zz))], dst.at[place(d)], sem, at_z(zz))

    to_heads(q_in, qg.at[y], sem_q.at[0], (0,) + FAR_FIRST, lambda d: rows(z * ROWS, ROWS))
    expect("q", qg.at[y], sem_q.at[0])

    stale_rows = rows(low * 128, 128)

    @pl.when(low != y)
    def _():
        for kv, src in enumerate((sk_in, sv_in)):
            remote(src.at[0, rows(y * 128, 128)], stale.at[sec, kv, stale_rows], sem_stale.at[0], (sec, sp, y))

    @pl.when(low == y)
    def _():
        for kv, src in enumerate((sk_in, sv_in)):
            pltpu.make_async_copy(src.at[0, rows(y * 128, 128)], stale.at[sec, kv, stale_rows], sem_stale.at[0]).start()

    for k in (1, 3, 2):
        yy = lax.rem(y + 4 - k, 4)
        await_(f"hop{k}")

        @pl.when(low != yy)
        def _():
            remote(hop.at[yy], stale.at[sec, :, stale_rows], sem_stale.at[0], (sec, sp, yy))

        @pl.when(low == yy)
        def _():
            pltpu.make_async_copy(hop.at[yy], stale.at[sec, :, stale_rows], sem_stale.at[0]).start()

    count[0] += 3 * 8
    expect("s", stale.at[sec], sem_stale.at[0])

    for name, i, distances in (("e", 0, (8, 6, 10, 4, 12, 2, 14, 0)), ("o", 1, (7, 9, 5, 11, 3, 13, 1, 15))):
        for kv, src in enumerate((fk_in, fv_in)):
            to_heads(src, fresh.at[sec, kv], sem_f.at[i], distances, lambda d: pl.ds((d % 2 * 8 + d // 2) * ROWS, ROWS))
        expect(name, fresh.at[sec, :, pl.ds(i * 256, 256)], sem_f.at[i])

    def text_rows(xx):
        return text.at[:, rows(xx * ROWS, ROWS)]

    text_mine = text_rows(x)

    @pl.when(high == x)
    def _():
        for kv, src in enumerate((tk_in, tv_in)):
            pltpu.make_async_copy(src.at[:, mine], text.at[kv, rows(x * ROWS, ROWS)], sem_text.at[0]).start()
            for d in (2, 1, 3):
                a = lax.rem(high + d, 4)
                there = text.at[kv, rows(x * ROWS, ROWS)]
                remote(src.at[:, cols(low * 4 + a)], there, sem_text.at[0], (sec, y * 4 + a, low))

    expect("t", text_mine, sem_text.at[0])

    text_to = [None] + [at_sec(lax.rem(x + d, 4) * 2 + core) for d in range(1, 4)]
    text_from = [None] + [text_rows(lax.rem(x + 4 - d, 4)) for d in range(1, 4)]

    def spread_text():
        await_("t")
        for d in (2, 1, 3):
            put(text_mine, text_mine, sem_text.at[d], text_to[d])
            expect(f"t{d}", text_from[d], sem_text.at[d])

    other = 1 - 2 * core
    left2, right2, opposite2 = left + other, right + other, opposite + other
    units = {"s": (stale, 0, 512, 0), "e": (fresh, 0, 256, 1), "o": (fresh, 256, 256, 2)}

    def part(u, s, half=None):
        ref, start, size, _ = units[u]
        if half is not None:
            start, size = start + half * size // 2, size // 2
        return ref.at[s, :, pl.ds(start, size)]

    def pass_on(u, i, ref, to, expected):
        sem = sem_u.at[units[u][3], i]
        put(ref, ref, sem, at_sec(to))
        expect(u + str(i), expected, sem)

    def spread(u):
        await_(u)
        block = part(u, sec)
        pass_on(u, 0, block, right, part(u, left))
        pass_on(u, 1, block, left, part(u, right))
        pass_on(u, 4, block, sibling, part(u, sibling))

    def forward(u):
        await_(u + "0")
        pass_on(u, 2, part(u, left, 0), right, part(u, opposite, 0))
        pass_on(u, 5, part(u, left), sibling, part(u, left2))
        await_(u + "1")
        pass_on(u, 3, part(u, right, 1), left, part(u, opposite, 1))
        pass_on(u, 6, part(u, right), sibling, part(u, right2))

    def forward_far(u):
        for i in range(2):
            await_(u + str(2 + i))
            pass_on(u, 7 + i, part(u, opposite, i), sibling, part(u, opposite2, i))

    def all_here(u):
        for i in range(4, 9):
            await_(u + str(i))

    vals2[:, HD:] = jnp.ones((KEYS, HD), jnp.bfloat16)
    await_("q")
    for k in (2, 1, 3):
        put(qg.at[y], qg.at[y], sem_y.at[k - 1], at_y(lax.rem(y + k, 4)))
        expect(f"q{k}", qg.at[lax.rem(y + 4 - k, 4)], sem_y.at[k - 1])
    spread("s")
    spread("e")
    for k in (1, 3, 2):
        await_(f"q{k}")
    for yy in range(4):
        wide = qg[yy].astype(jnp.float32) * SCALE2
        first = wide.astype(jnp.bfloat16)
        q2[yy, :, :HD] = first
        q2[yy, :, HD:] = (wide - first.astype(jnp.float32)).astype(jnp.bfloat16)
    forward("s")
    forward("e")
    forward_far("s")
    forward_far("e")
    spread("o")
    all_here("s")
    all_here("e")

    my_order = order[sec]

    def choose(i):
        for j in range(SEC):
            use_fresh = order[j] <= my_order
            block = pl.ds(i * HALF + j * 256, 256)
            here = pl.ds(i * 256, 256)
            chosen = jnp.where(use_fresh, fresh[j, 0, here, :], stale[j, 0, here, :])
            keys2[block, :HD] = chosen
            keys2[block, HD:] = chosen
            vals2[block, :HD] = jnp.where(use_fresh, fresh[j, 1, here, :], stale[j, 1, here, :])

    def tile_of(t):
        return lax.rem(y + 1 + t, 4), t // 4

    def scores(t, keys, slot):
        yy, half = tile_of(t)
        sbuf[slot, :, : keys.size] = lax.dot_general(
            q2[yy, rows(half * TILE, TILE), :], keys2[keys, :], (((1,), (1,)), ((), ())), preferred_element_type=jnp.float32
        )

    def weigh(keys, slot, best):
        weights = jnp.exp2(sbuf[slot, :, : keys.size] - best).astype(jnp.bfloat16)
        return jnp.dot(weights, vals2[keys, :], preferred_element_type=jnp.float32)

    def largest(keys, slot):
        return jnp.max(sbuf[slot, :, : keys.size], axis=1, keepdims=True)

    def begin(t, slot):
        best = largest(FIRST, slot)
        so_far[t] = weigh(FIRST, slot, best)
        best_so_far[t] = jnp.broadcast_to(best, (TILE, HD))

    def finish(t, slot):
        yy, half = tile_of(t)
        before = best_so_far[t]
        best = jnp.maximum(largest(SECOND, slot), before[:, :1])
        both = weigh(SECOND, slot, best)
        factor = jnp.exp2(before - best)
        total = both[:, HD:] + so_far[t, :, HD:] * factor
        value = (both[:, :HD] + so_far[t, :, :HD] * factor) / total
        return yy, half, value, best + jnp.log2(total)

    def end(t, slot):
        yy, half, value, level = finish(t, slot)
        partial[yy, rows(half * TILE, TILE), :] = value.astype(jnp.bfloat16)
        stats[yy, half] = jnp.transpose(level)[:8]
        own[half] = value
        own_l[half] = level

    def give(t):
        yy, half = tile_of(t)
        here = rows(half * TILE, TILE)
        remote(partial.at[yy, here], got.at[y, here], sem_part.at[half, y], at_y(yy))
        remote(stats.at[yy, half], got_stats.at[y, half], sem_stats.at[half, y], at_y(yy))

    def merge(half):
        here = pl.ds(half * TILE, TILE)
        levels, values = [own_l[half]], [own[half]]
        for k in (1, 3, 2):
            yy = lax.rem(y + k, 4)
            arrived(got.at[yy, here], sem_part.at[half, yy])
            arrived(got_stats.at[yy, half], sem_stats.at[half, yy])
            level = got_stats[yy, half]
            levels.append(jnp.transpose(jnp.broadcast_to(level[:1], (HD, TILE))))
            values.append(got[yy, here, :].astype(jnp.float32))
        top = jnp.maximum(jnp.maximum(levels[0], levels[1]), jnp.maximum(levels[2], levels[3]))
        shares = [jnp.exp2(level - top) for level in levels]
        total = shares[0] + shares[1] + shares[2] + shares[3]
        summed = shares[0] * values[0] + shares[1] * values[1] + shares[2] * values[2] + shares[3] * values[3]
        merged[here, :] = (summed / total).astype(jnp.bfloat16)
        for d in range(8):
            zz = half * 8 + d
            src = merged.at[pl.ds(zz * ROWS, ROWS)]

            @pl.when(zz == z)
            def _():
                pltpu.make_async_copy(src, out.at[:, mine], sem_out.at[0]).start()

            @pl.when(zz != z)
            def _():
                remote(src, out.at[:, mine], sem_out.at[0], at_z(zz))

    choose(0)
    scores(0, FIRST, 0)

    def pair_first(u, _):
        t = u * 2
        scores(t + 1, FIRST, 1)
        begin(t, 0)
        scores(t + 2, FIRST, 0)
        begin(t + 1, 1)
        return 0

    lax.fori_loop(0, 2, pair_first, 0)
    forward("o")
    spread_text()
    lax.fori_loop(2, 3, pair_first, 0)
    forward_far("o")
    scores(7, FIRST, 1)
    begin(6, 0)
    begin(7, 1)
    all_here("o")
    for d in range(1, 4):
        await_(f"t{d}")
    choose(1)
    keys2[2 * HALF :, :HD] = text[0]
    keys2[2 * HALF :, HD:] = text[0]
    vals2[2 * HALF :, :HD] = text[1]
    scores(0, SECOND, 0)

    def pair_second(u, _):
        t = u * 2
        scores(t + 1, SECOND, 1)
        end(t, 0)
        scores(t + 2, SECOND, 0)
        end(t + 1, 1)
        give(t)

        @pl.when(u != 1)
        def _():
            give(t + 1)

        return 0

    lax.fori_loop(0, 3, pair_second, 0)
    scores(7, SECOND, 1)
    end(6, 0)
    give(6)
    merge(0)
    end(7, 1)
    merge(1)

    arrived(out, sem_out.at[0])
    count[0] += 6 * 8 + 6 + 15
    assert not pending
    n, rest = divmod(count[0], 16)
    for _ in range(n):
        arrived(qg.at[0], sem_send.at[0])
    if rest:
        arrived(qg.at[0, pl.ds(0, rest * ROWS)], sem_send.at[0])

    @pl.when(high == x)
    def _():
        arrived(qg.at[0, pl.ds(0, 6 * ROWS)], sem_send.at[0])


def local(queries, fresh_keys, fresh_values, stale_keys, stale_values, text_keys, text_values, order):
    anywhere = pl.BlockSpec(memory_space=pl.ANY)
    dma = pltpu.SemaphoreType.DMA
    bf16, f32 = jnp.bfloat16, jnp.float32
    return pl.pallas_call(
        kernel,
        out_shape=jax.ShapeDtypeStruct((ROWS, 16 * HD), bf16),
        in_specs=[anywhere] * 7 + [pl.BlockSpec(memory_space=pltpu.SMEM)],
        out_specs=anywhere,
        scratch_shapes=[
            pltpu.VMEM((4, GROUP, HD), bf16),
            pltpu.VMEM((SEC, 2, GROUP, HD), bf16),
            pltpu.VMEM((SEC, 2, GROUP, HD), bf16),
            pltpu.VMEM((4, 2, 128, HD), bf16),
            pltpu.VMEM((2, TXT, HD), bf16),
            pltpu.VMEM((KEYS, 2 * HD), bf16),
            pltpu.VMEM((KEYS, 2 * HD), bf16),
            pltpu.VMEM((4, GROUP, 2 * HD), bf16),
            pltpu.VMEM((2, TILE, HALF + TXT), f32),
            pltpu.VMEM((8, TILE, 2 * HD), f32),
            pltpu.VMEM((8, TILE, HD), f32),
            pltpu.VMEM((4, GROUP, HD), bf16),
            pltpu.VMEM((4, 2, 8, TILE), f32),
            pltpu.VMEM((4, GROUP, HD), bf16),
            pltpu.VMEM((4, 2, 8, TILE), f32),
            pltpu.VMEM((2, TILE, HD), f32),
            pltpu.VMEM((2, TILE, HD), f32),
            pltpu.VMEM((GROUP, HD), bf16),
            dma((1,)),
            dma((1,)),
            dma((2,)),
            dma((4,)),
            dma((1,)),
            dma((3, 9)),
            dma((3,)),
            dma((3,)),
            dma((2, 4)),
            dma((2, 4)),
            dma((1,)),
        ],
        compiler_params=pltpu.CompilerParams(collective_id=0, has_side_effects=True, vmem_limit_bytes=56 << 20),
    )(queries, fresh_keys, fresh_values, stale_keys, stale_values, text_keys, text_values, order)


def solution(mesh):
    return jax.shard_map(
        local,
        mesh=mesh,
        in_specs=(
            P(("section", "sp", "cfg"), None),
            P(("section", "sp", "cfg"), None),
            P(("section", "sp", "cfg"), None),
            P("sp", ("section", "cfg"), None),
            P("sp", ("section", "cfg"), None),
            P("sp", None),
            P("sp", None),
            P(),
        ),
        out_specs=P(("section", "sp", "cfg"), None),
        check_vma=False,
    )
```

time: 98.4 us -> 81.8 us (0.83)
  Pallas kernels: 96.7 us -> 79.9 us
    pallas_call x1, Pallas kernels: 96.7 us -> 79.9 us  [local(): pl.pallas_call(kernel, out_shape=jax.ShapeDtypeStruct((ROWS, 16 * HD), bf...]
where the time goes in v3:
time: 81.8 us; the launch traced here: 81.5 us
  Pallas kernels  79.9 us (98%)
  local copies, waits for them, and re-layouts  1.57 us (2%)
    pallas_call x1, Pallas kernels, local(): pl.pallas_call(kernel, out_shape=jax.ShapeDtypeStruct((ROWS, 16 * HD), bf...  79.9 us

profile of v3, /device:TPU:1, one launch (start us, length us, event | category | flops | bytes accessed | tf_op | source)
XLA Modules:
  0.0 81.5 jit_solution(16021028893816880896)
XLA Ops:
  0.0 79.9 %shard_map.82 = bf16[32,2048]{1,0:T(8,128)(2,1)} custom-call(bf16[32,2048]{1,0:T(8,128)(2,1)} %q_in.1, bf16[32,2048]{1,0:T(8,128)(2,1)} %fk_in.1, bf16[32,2048]{1,0:T(8,128)(2,1)} %fv_in.1, bf16[1,512,128]{2,1,0:T(8,128)(2,1)} %sk_in.1, bf16[1,512,128]{2,1,0:T(8,128)(2,1)} %sv_in.1, bf16[32,2048]{1,0:T(8,128)(2,1)} %tk_in.1, bf16[32,2048]{1,0:T(8,128)(2,1)} %tv_in.1, ...), custom_call_target="tpu_custom_call" | custom-call | tf_op jit(solution)/shard_map/pallas_call | solution.py:390
  79.9 1.6 %copy.10 = bf16[32,2048]{1,0:T(8,128)(2,1)} copy(bf16[32,2048]{1,0:T(8,128)(2,1)} %shard_map.82) | data formatting | bytes 262144
